TPU v7x, 512 devices: a whole 4x8x8 slice. The times are simulated.
512 devices in a mesh: rep: 64 (over y_hi, z, x), tp: 8 (over y_lo, core).
Axes of the slice: x: 4, y: 8 (y_hi: 2, y_lo: 4; y = y_hi * 4 + y_lo), z: 8, core: 2. Of those that a mesh axis runs over, the one named last changes fastest.
Arguments:
- tokens: bfloat16 [24576, 12288], P('rep', 'tp'), may hold values from -6 to 6
- tenant: int32 [24576], P('rep'), may hold values from 0 to 2
- offsets: int32 [64], P('rep'), may hold values from 0 to 4095
- store_index: int32 [1], replicated, may hold values from 0 to 63
- frozen_key_weight: bfloat16 [12288, 1024], P('tp'), may hold values from -0.0546875 to 0.0546875
- store_a: float32 [64, 64, 12288], P('rep', None, 'tp'), may hold values from -0.0546875 to 0.0546875
- store_b: float32 [64, 1024, 64], P('rep', 'tp'), may hold values from -0.36 to 0.36
- bank_a: bfloat16 [64, 12288], P(None, 'tp'), may hold values from -0.0546875 to 0.0546875
- bank_b: bfloat16 [1024, 64], P('tp'), may hold values from -0.359375 to 0.359375
Outputs:
- key_rows: bfloat16 [24576, 1024], P('rep', 'tp')
Inputs may be any that keep to these rules, and one draw needn't show every extreme that they name: 0 marks a tenant without adapter, 1 the tenant of bank_a and bank_b, 2 the tenant whose adapter is merged.
All inputs are finite; a program needn't handle non-finite values.
Results may differ from a plain program's by a relative error of at most 0.0085.
Values may be sent and summed in bfloat16 or wider, within the bound.
A program may use at most 64 MiB of HBM per device.

v0:
```python
import math

import jax
import jax.numpy as jnp
from jax import lax
from jax.sharding import PartitionSpec as P

HEAD = 128


adapter_scale = 2.0


def spread(value, axis, source):
    kept = jnp.where(lax.axis_index(axis) == source, value, 0).astype(value.dtype)
    return lax.psum(kept, axis)


def rotate(heads, positions):
    half_width = heads.shape[-1] // 2
    inv_freq = jnp.exp(
        jnp.arange(half_width, dtype=jnp.float32) * (-2.0 * math.log(1000000.0) / heads.shape[-1])
    )
    angles = positions.astype(jnp.float32)[:, None] * inv_freq[None, :]
    cosine = jnp.cos(angles)[:, None, :]
    sine_vals = jnp.sin(angles)[:, None, :]
    leading = heads[..., :half_width]
    trailing = heads[..., half_width:]
    return jnp.concatenate(
        [leading * cosine - trailing * sine_vals, trailing * cosine + leading * sine_vals], axis=-1
    )


def per_device(
    tokens, tenant, offsets, store_index, frozen_key_weight, store_a, store_b, bank_a, bank_b
):
    root_index = store_index[0]
    factor_a, factor_b = (
        spread(store_a[0], "rep", root_index),
        spread(store_b[0], "rep", root_index),
    )
    up_full = lax.all_gather(factor_b, "tp", axis=0, tiled=True)
    weight_update = jnp.dot(factor_a.T, up_full.T, precision=lax.Precision.HIGHEST)
    merged_key_weight = (
        frozen_key_weight.astype(jnp.float32) + adapter_scale * weight_update
    ).astype(jnp.bfloat16)
    is_new = (tenant == 2)[:, None]
    blank = jnp.zeros_like(tokens)
    new_rows = jnp.where(is_new, tokens, blank)
    old_rows = jnp.where(is_new, blank, tokens)
    shrink_part = lax.dot_general(
        tokens, bank_a, (((1,), (1,)), ((), ())), preferred_element_type=jnp.float32
    )
    local_cols = bank_b.shape[0]
    row_total = tokens.shape[0]
    contract = (((0,), (1,)), ((), ()))
    projected_keys = lax.psum_scatter(
        lax.dot_general(frozen_key_weight, old_rows, contract, preferred_element_type=jnp.float32)
        + lax.dot_general(
            merged_key_weight, new_rows, contract, preferred_element_type=jnp.float32
        ),
        "tp",
        scatter_dimension=0,
        tiled=True,
    ).T
    shrink = lax.psum(shrink_part.astype(jnp.bfloat16), "tp").astype(jnp.float32)
    expand_factor = jnp.dot(shrink, bank_b.astype(jnp.float32).T, precision=lax.Precision.HIGHEST)
    adapted_keys = projected_keys + jnp.where(
        (tenant == 1)[:, None], adapter_scale * expand_factor, jnp.float32(0.0)
    )
    positions = offsets[0] + jnp.arange(row_total, dtype=jnp.int32)
    rotated = rotate(adapted_keys.reshape(row_total, local_cols // HEAD, HEAD), positions)
    return rotated.reshape(row_total, local_cols).astype(jnp.bfloat16)


def solution(mesh):
    in_specs = (
        P("rep", "tp"),
        P("rep"),
        P("rep"),
        P(),
        P("tp", None),
        P("rep", None, "tp"),
        P("rep", "tp", None),
        P(None, "tp"),
        P("tp", None),
    )
    out_specs = P("rep", "tp")
    return jax.shard_map(
        per_device, mesh=mesh, in_specs=in_specs, out_specs=out_specs, check_vma=False
    )
```

profile of v0, /device:TPU:1, one launch (start us, length us, event | category | flops | bytes accessed | tf_op | source)
XLA Modules:
  0.0 884.2 jit_solution(3474067942716101422)
XLA Ops:
  6.5 0.0 copy-start
  6.5 0.0 all-reduce.2.cloned.1.call-start
  7.2 0.8 select_bitcast_fusion
  8.0 0.0 all-reduce.2.cloned.1.call-update
  8.0 0.0 reduce-scatter.2.cloned.1.call-start
  8.1 391.8 %psum.22 = f32[128,64]{0,1:T(8,128)S(1)} all-reduce(f32[128,64]{0,1:T(8,128)S(1)} %select_bitcast_fusion.1), channel_id=1, replica_groups=mesh['rep'=64,'tp'=8] {'rep'}, use_global_device_ids=true, to_apply=%region_1.2 | all-reduce | flops 8192 | bytes 65536 | tf_op jit(solution)/shard_map/psum | solution.py:16
  399.9 68.0 %all_gather.3 = f32[1024,64]{0,1:T(8,128)S(1)} all-gather(f32[128,64]{0,1:T(8,128)S(1)} %psum.22), channel_id=1, replica_groups=mesh['rep'=64,'tp'=8] {'tp'}, dimensions={0}, use_global_device_ids=true | all-gather | bytes 294912 | tf_op jit(solution)/shard_map/all_gather | solution.py:42
  467.9 0.0 copy-done.4
  468.0 322.1 %all-reduce.2.cloned.1.call-done = f32[64,1536]{1,0:T(8,128)} async-done(((f32[64,1536]{1,0:T(8,128)}), f32[64,1536]{1,0:T(8,128)}) %all-reduce.2.cloned.1.call-update) | async-done | bytes 393232 | tf_op jit(solution)/shard_map/psum | solution.py:16
  790.0 7.1 add_convert_fusion
  797.1 0.0 copy-done.2
  797.1 0.0 copy-start.1
  797.1 1.9 fusion
  799.0 0.0 copy-done.1
  799.0 3.1 bitcast_add_fusion
  802.1 0.0 reduce-scatter.2.cloned.1.call-update
  802.8 0.0 copy-done
  802.8 0.4 convolution_convert_fusion
  803.2 60.6 %psum.23 = bf16[384,64]{1,0:T(8,128)(2,1)S(1)} all-reduce(bf16[384,64]{1,0:T(8,128)(2,1)S(1)} %convolution_convert_fusion), channel_id=1, replica_groups=mesh['rep'=64,'tp'=8] {'tp'}, use_global_device_ids=true, to_apply=%region_3.4 | all-reduce | flops 24576 | bytes 98304 | tf_op jit(solution)/shard_map/psum | solution.py:66
  863.9 11.0 %reduce-scatter.2.cloned.1.call-done = f32[128,384]{1,0:T(8,128)} async-done(((f32[1024,384]{1,0:T(8,128)}), f32[128,384]{1,0:T(8,128)}) %reduce-scatter.2.cloned.1.call-update) | async-done | bytes 196624 | tf_op jit(solution)/shard_map/reduce_scatter | solution.py:57
  874.9 0.0 copy-done.3
  874.9 1.1 fusion.7
  876.1 0.4 fusion.15
  876.6 0.8 copy.13
  (8 shorter events, 0.1 us)
Async XLA Ops:
  6.5 796.3 %copy-start = (bf16[64,1536]{1,0:T(8,128)(2,1)S(1)}, bf16[64,1536]{1,0:T(8,128)(2,1)}, u32[]{:S(2)}) copy-start(bf16[64,1536]{1,0:T(8,128)(2,1)} %param.16) | copy-start | bytes 589828
  6.5 461.4 %copy-start.4 = (s32[384]{0:T(512)S(1)}, s32[384]{0:T(512)}, u32[]{:S(2)}) copy-start(s32[384]{0:T(512)} %param.10) | copy-start | bytes 4612
  6.5 783.5 %all-reduce.2.cloned.1.call-start = ((), (), s32[]{:S(2)}) async-start(), calls=%async_computation.1 | async-start | bytes 786432 | tf_op jit(solution)/shard_map/psum | solution.py:16
  8.0 866.9 %reduce-scatter.2.cloned.1.call-start = ((), (), s32[]{:S(2)}) async-start(), calls=%async_computation.2 | async-start | bytes 1769472 | tf_op jit(solution)/shard_map/reduce_scatter | solution.py:57
  467.9 329.1 %copy-start.2 = (bf16[384,1536]{1,0:T(8,128)(2,1)S(1)}, bf16[384,1536]{1,0:T(8,128)(2,1)}, u32[]{:S(2)}) copy-start(bf16[384,1536]{1,0:T(8,128)(2,1)} %param.9) | copy-start | bytes 3538948
  797.1 2.0 copy-start.1
  802.1 72.8 %copy-start.3 = (bf16[128,64]{0,1:T(8,128)(2,1)S(1)}, bf16[128,64]{0,1:T(8,128)(2,1)}, u32[]{:S(2)}) copy-start(bf16[128,64]{0,1:T(8,128)(2,1)} %param.17) | copy-start | bytes 49156
Sparse Core Ops, SparseCore 0:
  10.3 779.6 all-reduce.1
  802.3 72.6 reduce-scatter.1
where the time goes:
time: 886 us; the launch traced here: 884 us
  blocking collectives  520 us (59%)
  waiting for transfers between devices  333 us (38%)
  between operations  14.9 us (2%)
  matrix products  13.6 us (2%)
    psum x1, blocking collectives, spread(): return lax.psum(kept, axis)  392 us
    psum x1, waiting for transfers between devices, spread(): return lax.psum(kept, axis)  322 us
    all_gather x1, blocking collectives, per_device(): up_full = lax.all_gather(factor_b, 'tp', axis=0, tiled=True)  68 us
    psum x1, blocking collectives, per_device(): lax.psum(shrink_part.astype(jnp.bfloat16), 'tp').astype(jnp.float32)  60.6 us
  transfers between devices with their start and end apart: 2, of which 2 were waited for; matrix products, arithmetic and copies ran while one was open for 0% of the time, Pallas kernels for 0%

commit v1 on v0

v1 whole, which is shorter than its diff:
```python
import functools
import math

import jax
import jax.numpy as jnp
from jax import lax
from jax.experimental import pallas as pl
from jax.experimental.pallas import tpu as pltpu
from jax.sharding import PartitionSpec as P

MESH = pl.DeviceIdType.MESH
SCALE = 2.0
NY, NZ, NX = 2, 8, 4
NT = 8
ROWS = 384
FEAT = 1536
HEAD = 128
RANK = 64
PART = ROWS // NT
TILES = 7
SLICE = 16 * TILES


def kernel(
    index_ref, offset_ref, tenant_ref, tok_hbm, w_hbm, a_hbm, bt_hbm, ba_hbm, bbt_hbm, out_ref,
    tok, w, a_raw, bt_raw, ranks, ups,
    z_src, z_got, x_got, y_got, g_got,
    part_src, part_got, low_src, low_got, low_sum,
    acc, cos2, sin2,
    load_sem, z_ss, z_rs, x_ss, x_rs, y_ss, y_rs, g_ss, g_rs, p_ss, p_rs, s_ss, s_rs, t_ss, t_rs,
):
    rep, t = lax.axis_index("rep"), lax.axis_index("tp")
    yh, z, x = rep // (NZ * NX), (rep // NX) % NZ, rep % NX

    def at(yh_, z_, x_):
        return (yh_ * NZ + z_) * NX + x_

    z_of = [(z + k) % NZ for k in range(1, NZ)]
    x_of = [(x + k) % NX for k in range(1, NX)]
    t_of = [(t + k) % NT for k in range(1, NT)]
    z_peers = [(at(yh, q, x), t) for q in z_of]
    x_peers = [(at(yh, z, q), t) for q in x_of]
    y_peer = (at(1 - yh, z, x), t)
    t_peers = [(rep, q) for q in t_of]

    barrier = pltpu.get_barrier_semaphore()
    peers = z_peers + x_peers + [y_peer] + t_peers
    for peer in peers:
        pl.semaphore_signal(barrier, inc=1, device_id=peer, device_id_type=MESH)

    loads = [
        pltpu.make_async_copy(src, dst, load_sem.at[i])
        for i, (src, dst) in enumerate(
            [
                (a_hbm, a_raw),
                (bt_hbm, bt_raw),
                (tok_hbm, tok),
                (w_hbm, w),
                (ba_hbm, ranks.at[pl.ds(0, RANK)]),
                (bbt_hbm, ups.at[pl.ds(0, RANK)]),
            ]
        )
    ]
    for load in loads:
        load.start()

    root = index_ref[0]
    root_y, root_z, root_x = root // (NZ * NX), (root // NX) % NZ, root % NX

    loads[0].wait()
    loads[1].wait()
    for q in range(NZ):
        block, half = q // 2, q % 2
        for j in range(TILES - 1):
            column = (half * (TILES - 1) + j) * HEAD
            z_src[q, 16 * j : 16 * (j + 1), :] = a_raw[
                16 * block : 16 * (block + 1), column : column + HEAD
            ].astype(jnp.bfloat16)
        z_src[q, 16 * (TILES - 1) :, :] = bt_raw[16 * block : 16 * (block + 1), :].astype(jnp.bfloat16)

    pl.semaphore_wait(barrier, len(peers))

    def send(src, dst, ss, rs, peer):
        copy = pltpu.make_async_remote_copy(
            src_ref=src, dst_ref=dst, send_sem=ss, recv_sem=rs, device_id=peer, device_id_type=MESH
        )
        copy.start()
        return copy

    sent = []
    z_copies = [
        send(z_src.at[z_of[i]], z_got.at[z], z_ss.at[i], z_rs.at[i], z_peers[i]) for i in range(NZ - 1)
    ]
    z_got[z] = z_src[z]

    loads[2].wait()
    loads[3].wait()
    p_copies = []
    for k in range(1, NT):
        q = t_of[k - 1]
        column = pl.multiple_of(q * HEAD, HEAD)
        part_src[k - 1] = jnp.dot(
            tok[...], w[:, pl.ds(column, HEAD)], preferred_element_type=jnp.float32
        ).astype(jnp.bfloat16)
        p_copies.append(
            send(part_src.at[k - 1], part_got.at[k - 1], p_ss.at[k - 1], p_rs.at[k - 1], t_peers[k - 1])
        )

    for copy in z_copies:
        copy.wait_recv()
    x_got[x] = z_got[root_z]
    x_copies = [
        send(x_got.at[x], x_got.at[x], x_ss.at[i], x_rs.at[i], x_peers[i]) for i in range(NX - 1)
    ]
    acc[...] = jnp.dot(
        tok[...],
        w[:, pl.ds(pl.multiple_of(t * HEAD, HEAD), HEAD)],
        preferred_element_type=jnp.float32,
    )
    for copy in x_copies:
        copy.wait_recv()
    y_got[yh] = x_got[root_x]
    y_copy = send(y_got.at[yh], y_got.at[yh], y_ss, y_rs, y_peer)

    lane = lax.broadcasted_iota(jnp.int32, (ROWS, HEAD), 1)
    row = lax.broadcasted_iota(jnp.int32, (ROWS, HEAD), 0)
    pair = (lane % (HEAD // 2)).astype(jnp.float32)
    freq = jnp.exp(pair * (-2.0 * math.log(1000000.0) / HEAD))
    angle = (offset_ref[0] + row).astype(jnp.float32) * freq
    cos2[...] = jnp.cos(angle)
    sine = jnp.sin(angle)
    sin2[...] = jnp.where(lane < HEAD // 2, -sine, sine)

    y_copy.wait_recv()
    g_got[z] = y_got[root_y]
    g_copies = [
        send(g_got.at[z], g_got.at[z], g_ss.at[i], g_rs.at[i], z_peers[i]) for i in range(NZ - 1)
    ]
    total = acc[...]
    for i, copy in enumerate(p_copies):
        copy.wait_recv()
        total = total + part_got[i].astype(jnp.float32)
    acc[...] = total
    loads[4].wait()
    loads[5].wait()

    eye = lax.broadcasted_iota(jnp.int32, (HEAD, HEAD), 0) == lax.broadcasted_iota(
        jnp.int32, (HEAD, HEAD), 1
    )
    columns = [
        jnp.sum(
            jnp.where(eye, tenant_ref[:, HEAD * i : HEAD * (i + 1)], 0).astype(jnp.float32),
            axis=1,
            keepdims=True,
        )
        for i in range(ROWS // HEAD)
    ]
    tenant = jnp.concatenate(columns, axis=0)
    wanted = jnp.where(lane < RANK, 1.0, 2.0)

    for copy in g_copies:
        copy.wait_recv()
    for q in range(NZ):
        block, half = q // 2, q % 2
        for j in range(TILES - 1):
            column = (half * (TILES - 1) + j) * HEAD
            ranks[RANK + 16 * block : RANK + 16 * (block + 1), column : column + HEAD] = g_got[
                q, 16 * j : 16 * (j + 1), :
            ]
        if half == 0:
            ups[RANK + 16 * block : RANK + 16 * (block + 1), :] = g_got[q, 16 * (TILES - 1) :, :]
    low = lax.dot_general(
        tok[...], ranks[...], (((1,), (1,)), ((), ())), preferred_element_type=jnp.float32
    )
    low_src[...] = jnp.where(tenant == wanted, low, 0.0).astype(jnp.bfloat16)

    def rows_of(q):
        return pl.ds(pl.multiple_of(q * PART, 16), PART)

    s_copies = [
        send(low_src.at[rows_of(t_of[i])], low_got.at[i], s_ss.at[i], s_rs.at[i], t_peers[i])
        for i in range(NT - 1)
    ]
    total = low_src[rows_of(t), :].astype(jnp.float32)
    for i, copy in enumerate(s_copies):
        copy.wait_recv()
        total = total + low_got[i].astype(jnp.float32)
    low_sum[rows_of(t), :] = total.astype(jnp.bfloat16)
    t_copies = [
        send(low_sum.at[rows_of(t)], low_sum.at[rows_of(t)], t_ss.at[i], t_rs.at[i], t_peers[i])
        for i in range(NT - 1)
    ]
    for copy in z_copies + p_copies + x_copies + [y_copy] + g_copies + s_copies:
        copy.wait_send()
    for copy in t_copies:
        copy.wait_recv()
    adapted = acc[...] + SCALE * jnp.dot(low_sum[...], ups[...], preferred_element_type=jnp.float32)
    swapped = pltpu.roll(adapted, HEAD // 2, 1)
    out_ref[...] = (adapted * cos2[...] + swapped * sin2[...]).astype(jnp.bfloat16)
    for copy in t_copies:
        copy.wait_send()


def per_device(
    tokens, tenant, offsets, store_index, frozen_key_weight, store_a, store_b, bank_a, bank_b
):
    bf16, f32 = jnp.bfloat16, jnp.float32
    smem = pl.BlockSpec(memory_space=pltpu.SMEM)
    vmem = pl.BlockSpec(memory_space=pltpu.VMEM)
    hbm = pl.BlockSpec(memory_space=pl.ANY)
    dma = pltpu.SemaphoreType.DMA
    return pl.pallas_call(
        kernel,
        out_shape=jax.ShapeDtypeStruct((ROWS, HEAD), bf16),
        in_specs=[smem, smem, vmem] + [hbm] * 6,
        out_specs=vmem,
        scratch_shapes=[
            pltpu.VMEM((ROWS, FEAT), bf16),
            pltpu.VMEM((FEAT, NT * HEAD), bf16),
            pltpu.VMEM((RANK, FEAT), f32),
            pltpu.VMEM((RANK, HEAD), f32),
            pltpu.VMEM((2 * RANK, FEAT), bf16),
            pltpu.VMEM((2 * RANK, HEAD), bf16),
            pltpu.VMEM((NZ, SLICE, HEAD), bf16),
            pltpu.VMEM((NZ, SLICE, HEAD), bf16),
            pltpu.VMEM((NX, SLICE, HEAD), bf16),
            pltpu.VMEM((NY, SLICE, HEAD), bf16),
            pltpu.VMEM((NZ, SLICE, HEAD), bf16),
            pltpu.VMEM((NT - 1, ROWS, HEAD), bf16),
            pltpu.VMEM((NT - 1, ROWS, HEAD), bf16),
            pltpu.VMEM((ROWS, 2 * RANK), bf16),
            pltpu.VMEM((NT - 1, PART, 2 * RANK), bf16),
            pltpu.VMEM((ROWS, 2 * RANK), bf16),
            pltpu.VMEM((ROWS, HEAD), f32),
            pltpu.VMEM((ROWS, HEAD), f32),
            pltpu.VMEM((ROWS, HEAD), f32),
            dma((6,)),
            dma((NZ - 1,)), dma((NZ - 1,)),
            dma((NX - 1,)), dma((NX - 1,)),
            dma, dma,
            dma((NZ - 1,)), dma((NZ - 1,)),
            dma((NT - 1,)), dma((NT - 1,)),
            dma((NT - 1,)), dma((NT - 1,)),
            dma((NT - 1,)), dma((NT - 1,)),
        ],
        compiler_params=pltpu.CompilerParams(
            collective_id=0, has_side_effects=True, vmem_limit_bytes=60 * 1024 * 1024
        ),
        name="key_rows",
    )(
        store_index,
        offsets,
        tenant.reshape(1, ROWS),
        tokens,
        frozen_key_weight,
        store_a[0],
        store_b[0].T,
        bank_a,
        bank_b.T,
    )


def solution(mesh):
    in_specs = (
        P("rep", "tp"),
        P("rep"),
        P("rep"),
        P(),
        P("tp", None),
        P("rep", None, "tp"),
        P("rep", "tp", None),
        P(None, "tp"),
        P("tp", None),
    )
    return jax.shard_map(
        per_device, mesh=mesh, in_specs=in_specs, out_specs=P("rep", "tp"), check_vma=False
    )
```

time: 886 us -> 53.9 us (0.06)
  blocking collectives: 520 us -> 0 us
  waiting for transfers between devices: 333 us -> 0 us
  Pallas kernels: 0 us -> 49.6 us
  matrix products: 13.6 us -> 0 us
  between operations: 14.9 us -> 1.31 us
    psum x2 -> x0, blocking collectives: 452 us -> none  [the longest x1 392 us: spread(): return lax.psum(kept, axis)]
    psum x1 -> x0, waiting for transfers between devices: 322 us -> none  [spread(): return lax.psum(kept, axis)]
    all_gather x1 -> x0, blocking collectives: 68 us -> none  [per_device(): up_full = lax.all_gather(factor_b, 'tp', axis=0, tiled=True)]
    pallas_call x0 -> x1, Pallas kernels: none -> 49.6 us  [per_device(): pl.pallas_call(kernel, out_shape=jax.ShapeDtypeStruct((ROWS, HEAD), bf16)...]
    dot_general x5 -> x0, matrix products: 13.6 us -> none  [the longest x1 7.05 us: per_device(): jnp.dot(factor_a.T, up_full.T, precision=lax.Precision.HIGHEST)]
    reduce_scatter x1 -> x0, waiting for transfers between devices: 11 us -> none  [per_device(): lax.psum_scatter(lax.dot_general(frozen_key_weight, old_rows, contract, p...]
  transfers between devices with their start and end apart: 2 -> 0, of which waited for: 2 -> 0; matrix products, arithmetic and copies ran while one was open for 0% -> 0% of each run, Pallas kernels for 0% -> 0%
where the time goes in v1:
time: 53.9 us; the launch traced here: 53.7 us
  Pallas kernels  49.6 us (92%)
  local copies, waits for them, and re-layouts  2.79 us (5%)
  between operations  1.31 us (2%)
    pallas_call x1, Pallas kernels, per_device(): pl.pallas_call(kernel, out_shape=jax.ShapeDtypeStruct((ROWS, HEAD), bf16)...  49.6 us
    unnamed x1, local copies, waits for them, and re-layouts  1.54 us
    reshape x1, local copies, waits for them, and re-layouts, per_device(): tenant.reshape(1, ROWS)  1.25 us

profile of v1, /device:TPU:1, one launch (start us, length us, event | category | flops | bytes accessed | tf_op | source)
XLA Modules:
  0.0 53.7 jit_solution(8639083360788758584)
XLA Ops:
  1.3 1.2 %reshape.3.tenant_ref = s32[1,384]{1,0:T(1,128)} reshape(s32[384]{0:T(512)} %param.10) | data formatting | bytes 3072 | tf_op jit(solution)/shard_map/reshape | solution.py:253
  2.5 49.6 %key_rows.1 = bf16[384,128]{1,0:T(8,128)(2,1)} custom-call(s32[1]{0:T(128)S(6)} %copy.12.index_ref, s32[1]{0:T(128)S(6)} %copy.11.offset_ref, s32[1,384]{1,0:T(1,128)} %reshape.3.tenant_ref, bf16[384,1536]{1,0:T(8,128)(2,1)} %tok_hbm.1, bf16[1536,1024]{1,0:T(8,128)(2,1)} %w_hbm.1, f32[64,1536]{1,0:T(8,128)} %bitcast.5, f32[64,128]{1,0:T(8,128)} %bitcast.6, ...), custom_call_target="tpu_custom_call" | custom-call | tf_op jit(solution)/shard_map/key_rows/pallas_call | solution.py:212
  52.1 1.5 %copy.13 = bf16[384,128]{1,0:T(8,128)(2,1)} copy(bf16[384,128]{1,0:T(8,128)(2,1)} %key_rows.1) | data formatting | bytes 196608

commit v2 on v1

v2 whole, which is shorter than its diff:
```python
import math

import jax
import jax.numpy as jnp
from jax import lax
from jax.experimental import pallas as pl
from jax.experimental.pallas import tpu as pltpu
from jax.sharding import PartitionSpec as P

MESH = pl.DeviceIdType.MESH
SCALE = 2.0
NY, NZ, NX = 2, 8, 4
NC = 4
ROWS = 384
FEAT = 1536
HEAD = 128
RANK = 64
HALF = ROWS // 2
PACK = ROWS // 4
TILES = (4, 3)
CHUNK = FEAT // 2


def kernel(
    index_ref, offset_ref, tenant_ref, tok_hbm, w_hbm, a_hbm, bt_hbm, ba_hbm, bbt_hbm, out_ref,
    tok, w, a_raw, bt_raw, bank, ranks, bank_up, up,
    z_src0, z_src1, z_got0, z_got1, x_got0, x_got1, y_got0, y_got1, g_got0, g_got1,
    mine, pair_src, pair_got, part_src, part_got,
    l_mine, l_src, l_got, l_chip, l_chips, l_all,
    acc, cos2, sin2,
    load_sem, z_ss, z_rs, x_ss, x_rs, y_ss, y_rs, g_ss, g_rs, q_ss, q_rs, p_ss, p_rs, l_ss, l_rs,
):
    bf16, f32 = jnp.bfloat16, jnp.float32
    rep, t = lax.axis_index("rep"), lax.axis_index("tp")
    yh, z, x = rep // (NZ * NX), (rep // NX) % NZ, rep % NX
    yl, core = t // 2, t % 2

    def at(yh_, z_, x_):
        return (yh_ * NZ + z_) * NX + x_

    z_of = [(z + k) % NZ for k in range(1, NZ)]
    x_of = [(x + k) % NX for k in range(1, NX)]
    c_of = [(yl + k) % NC for k in range(1, NC)]
    z_peers = [(at(yh, q, x), t) for q in z_of]
    x_peers = [(at(yh, z, q), t) for q in x_of]
    y_peer = (at(1 - yh, z, x), t)
    c_peers = [(rep, 2 * q + core) for q in c_of]
    twin = (rep, 2 * yl + 1 - core)

    barrier = pltpu.get_barrier_semaphore()
    peers = z_peers + x_peers + [y_peer] + c_peers + [twin]
    for peer in peers:
        pl.semaphore_signal(barrier, inc=1, device_id=peer, device_id_type=MESH)

    bank_up[...] = jnp.zeros_like(bank_up)
    up[...] = jnp.zeros_like(up)
    loads = [
        pltpu.make_async_copy(src, dst, load_sem.at[i])
        for i, (src, dst) in enumerate(
            [
                (a_hbm, a_raw),
                (bt_hbm, bt_raw),
                (tok_hbm, tok),
                (ba_hbm, bank.at[pl.ds(0, RANK)]),
                (ba_hbm, bank.at[pl.ds(RANK, RANK)]),
                (w_hbm, w),
                (bbt_hbm, bank_up.at[pl.ds(0, RANK), pl.ds(0, HEAD)]),
                (bbt_hbm, bank_up.at[pl.ds(RANK, RANK), pl.ds(HEAD, HEAD)]),
            ]
        )
    ]
    for load in loads:
        load.start()

    root = index_ref[0]
    root_y, root_z, root_x = root // (NZ * NX), (root // NX) % NZ, root % NX

    z_src, z_got, x_got, y_got, g_got = (
        (z_src0, z_src1), (z_got0, z_got1), (x_got0, x_got1), (y_got0, y_got1), (g_got0, g_got1)
    )

    def tile(q, chunk, j):
        return 16 * (q // 2), chunk * CHUNK + ((q % 2) * 3 + j) * HEAD

    loads[0].wait()
    loads[1].wait()
    for chunk in range(2):
        for q in range(NZ):
            for j in range(3):
                row, column = tile(q, chunk, j)
                z_src[chunk][q, 16 * j : 16 * (j + 1), :] = a_raw[
                    row : row + 16, column : column + HEAD
                ].astype(bf16)
            if chunk == 0:
                row = 16 * (q // 2)
                z_src[chunk][q, 48:64, :] = bt_raw[row : row + 16, :].astype(bf16)

    pl.semaphore_wait(barrier, len(peers))

    started = []

    def send(src, dst, ss, rs, peer):
        copy = pltpu.make_async_remote_copy(
            src_ref=src, dst_ref=dst, send_sem=ss, recv_sem=rs, device_id=peer, device_id_type=MESH
        )
        copy.start()
        started.append(copy)
        return copy

    def arrived(copies):
        for copy in copies:
            copy.wait_recv()

    z_copies = [
        [
            send(
                z_src[chunk].at[z_of[i]], z_got[chunk].at[z],
                z_ss.at[chunk, i], z_rs.at[chunk, i], z_peers[i],
            )
            for i in range(NZ - 1)
        ]
        for chunk in range(2)
    ]
    for chunk in range(2):
        z_got[chunk][z] = z_src[chunk][z]

    lane = lax.broadcasted_iota(jnp.int32, (PACK, HEAD), 1)
    left = lane < RANK

    def low_start(s, low):
        halves = [
            jnp.where(left, low[HALF * h : HALF * h + PACK], low[HALF * h + PACK : HALF * (h + 1)])
            for h in range(2)
        ]
        l_mine[s] = jnp.where(core == 0, halves[0], halves[1])
        l_src[s] = jnp.where(core == 0, halves[1], halves[0]).astype(bf16)
        return send(l_src.at[s], l_got.at[s], l_ss.at[s, 0], l_rs.at[s, 0], twin)

    def low_spread(s, copy):
        copy.wait_recv()
        l_chip[s] = (l_mine[s] + l_got[s].astype(f32)).astype(bf16)
        return [
            send(l_chip.at[s], l_chips.at[s, i], l_ss.at[s, 1 + i], l_rs.at[s, 1 + i], c_peers[i])
            for i in range(NC - 1)
        ]

    def low_join(s, copies):
        total = l_chip[s].astype(f32)
        for i, copy in enumerate(copies):
            copy.wait_recv()
            total = total + l_chips[s, i].astype(f32)
        l_all[s, core] = total.astype(bf16)
        return send(l_all.at[s, core], l_all.at[s, core], l_ss.at[s, NC], l_rs.at[s, NC], twin)

    def expanded(s, copy, ups):
        copy.wait_recv()
        parts = []
        for h in range(2):
            both = jnp.dot(l_all[s, h], ups[...], preferred_element_type=f32)
            parts += [both[:, :HEAD], both[:, HEAD:]]
        return SCALE * jnp.concatenate(parts, axis=0)

    def times_ranks(a, b):
        return lax.dot_general(a, b, (((1,), (1,)), ((), ())), preferred_element_type=f32)

    loads[2].wait()
    loads[3].wait()
    loads[4].wait()
    bank_step = low_start(0, times_ranks(tok[...], bank[...]))

    loads[5].wait()
    order = c_of + [yl]
    pair_copies = []
    part_copies = []

    def passed(k):
        pair_copies[k].wait_recv()
        total = mine[k] + pair_got[k].astype(f32)
        if k == NC - 1:
            acc[...] = total
            return
        part_src[k] = total.astype(bf16)
        part_copies.append(
            send(part_src.at[k], part_got.at[k], p_ss.at[k], p_rs.at[k], c_peers[k])
        )

    for k, q in enumerate(order):
        column = pl.multiple_of(q * 2 * HEAD, 2 * HEAD)
        both = jnp.dot(tok[...], w[:, pl.ds(column, 2 * HEAD)], preferred_element_type=f32)
        mine[k] = jnp.where(core == 0, both[:, :HEAD], both[:, HEAD:])
        pair_src[k] = jnp.where(core == 0, both[:, HEAD:], both[:, :HEAD]).astype(bf16)
        pair_copies.append(send(pair_src.at[k], pair_got.at[k], q_ss.at[k], q_rs.at[k], twin))
        if k == 1:
            bank_step = low_spread(0, bank_step)
        if k >= 1:
            passed(k - 1)
    passed(NC - 1)

    wide = lax.broadcasted_iota(jnp.int32, (HALF, HEAD), 1)
    row = lax.broadcasted_iota(jnp.int32, (HALF, HEAD), 0)
    row = jnp.where(wide < HEAD // 2, row, row + HALF)
    freq = jnp.exp((wide % (HEAD // 2)).astype(f32) * (-2.0 * math.log(1000000.0) / HEAD))
    angle = (offset_ref[0] + row).astype(f32) * freq
    first = wide < HEAD // 2
    cosine, sine = jnp.cos(angle), jnp.sin(angle)
    turned_cos, turned_sin = pltpu.roll(cosine, HEAD // 2, 1), pltpu.roll(sine, HEAD // 2, 1)
    cos2[0:HALF, :] = jnp.where(first, cosine, turned_cos)
    cos2[HALF:, :] = jnp.where(first, turned_cos, cosine)
    sin2[0:HALF, :] = jnp.where(first, -sine, turned_sin)
    sin2[HALF:, :] = jnp.where(first, -turned_sin, sine)

    x_copies, y_copies, g_copies = [], [], []
    for chunk in range(2):
        arrived(z_copies[chunk])
        x_got[chunk][x] = z_got[chunk][root_z]
        x_copies.append(
            [
                send(
                    x_got[chunk].at[x], x_got[chunk].at[x],
                    x_ss.at[chunk, i], x_rs.at[chunk, i], x_peers[i],
                )
                for i in range(NX - 1)
            ]
        )
    for chunk in range(2):
        arrived(x_copies[chunk])
        y_got[chunk][yh] = x_got[chunk][root_x]
        y_copies.append(
            send(y_got[chunk].at[yh], y_got[chunk].at[yh], y_ss.at[chunk], y_rs.at[chunk], y_peer)
        )
    bank_step = low_join(0, bank_step)

    eye = lax.broadcasted_iota(jnp.int32, (HEAD, HEAD), 0) == lax.broadcasted_iota(
        jnp.int32, (HEAD, HEAD), 1
    )
    tenant = jnp.concatenate(
        [
            jnp.sum(
                jnp.where(eye, tenant_ref[pl.ds(HEAD * i, HEAD)].reshape(1, HEAD), 0).astype(f32),
                axis=1,
                keepdims=True,
            )
            for i in range(ROWS // HEAD)
        ],
        axis=0,
    )

    for chunk in range(2):
        y_copies[chunk].wait_recv()
        g_got[chunk][z] = y_got[chunk][root_y]
        g_copies.append(
            [
                send(
                    g_got[chunk].at[z], g_got[chunk].at[z],
                    g_ss.at[chunk, i], g_rs.at[chunk, i], z_peers[i],
                )
                for i in range(NZ - 1)
            ]
        )

    total = acc[...]
    for k, copy in enumerate(part_copies):
        copy.wait_recv()
        total = total + part_got[k].astype(f32)
    loads[6].wait()
    loads[7].wait()
    acc[...] = total + jnp.where(tenant == 1.0, expanded(0, bank_step, bank_up), 0.0)

    low = None
    for chunk in range(2):
        arrived(g_copies[chunk])
        for q in range(NZ):
            for j in range(3):
                row, column = tile(q, chunk, j)
                value = g_got[chunk][q, 16 * j : 16 * (j + 1), :]
                ranks[row : row + 16, column : column + HEAD] = value
                ranks[RANK + row : RANK + row + 16, column : column + HEAD] = value
        columns = slice(chunk * CHUNK, (chunk + 1) * CHUNK)
        term = times_ranks(tok[:, columns], ranks[:, columns])
        low = term if low is None else low + term
    store_step = low_start(1, low)
    for q in range(0, NZ, 2):
        row = 16 * (q // 2)
        value = g_got[0][q, 48:64, :]
        up[row : row + 16, 0:HEAD] = value
        up[RANK + row : RANK + row + 16, HEAD:] = value
    store_step = low_spread(1, store_step)
    store_step = low_join(1, store_step)
    adapted = acc[...] + jnp.where(tenant == 2.0, expanded(1, store_step, up), 0.0)
    swapped = pltpu.roll(adapted, HEAD // 2, 1)
    out_ref[...] = (adapted * cos2[...] + swapped * sin2[...]).astype(bf16)
    for copy in started:
        copy.wait_send()


def per_device(
    tokens, tenant, offsets, store_index, frozen_key_weight, store_a, store_b, bank_a, bank_b
):
    bf16, f32 = jnp.bfloat16, jnp.float32
    smem = pl.BlockSpec(memory_space=pltpu.SMEM)
    vmem = pl.BlockSpec(memory_space=pltpu.VMEM)
    hbm = pl.BlockSpec(memory_space=pl.ANY)
    dma = pltpu.SemaphoreType.DMA

    def slices(n):
        return [pltpu.VMEM((n, 16 * tiles, HEAD), bf16) for tiles in TILES]

    return pl.pallas_call(
        kernel,
        out_shape=jax.ShapeDtypeStruct((ROWS, HEAD), bf16),
        in_specs=[smem, smem, vmem] + [hbm] * 6,
        out_specs=vmem,
        scratch_shapes=[
            pltpu.VMEM((ROWS, FEAT), bf16),
            pltpu.VMEM((FEAT, 2 * NC * HEAD), bf16),
            pltpu.VMEM((RANK, FEAT), f32),
            pltpu.VMEM((RANK, HEAD), f32),
            pltpu.VMEM((2 * RANK, FEAT), bf16),
            pltpu.VMEM((2 * RANK, FEAT), bf16),
            pltpu.VMEM((2 * RANK, 2 * HEAD), bf16),
            pltpu.VMEM((2 * RANK, 2 * HEAD), bf16),
            *slices(NZ), *slices(NZ), *slices(NX), *slices(NY), *slices(NZ),
            pltpu.VMEM((NC, ROWS, HEAD), f32),
            pltpu.VMEM((NC, ROWS, HEAD), bf16),
            pltpu.VMEM((NC, ROWS, HEAD), bf16),
            pltpu.VMEM((NC - 1, ROWS, HEAD), bf16),
            pltpu.VMEM((NC - 1, ROWS, HEAD), bf16),
            pltpu.VMEM((2, PACK, HEAD), f32),
            pltpu.VMEM((2, PACK, HEAD), bf16),
            pltpu.VMEM((2, PACK, HEAD), bf16),
            pltpu.VMEM((2, PACK, HEAD), bf16),
            pltpu.VMEM((2, NC - 1, PACK, HEAD), bf16),
            pltpu.VMEM((2, 2, PACK, HEAD), bf16),
            pltpu.VMEM((ROWS, HEAD), f32),
            pltpu.VMEM((ROWS, HEAD), f32),
            pltpu.VMEM((ROWS, HEAD), f32),
            dma((8,)),
            dma((2, NZ - 1)), dma((2, NZ - 1)),
            dma((2, NX - 1)), dma((2, NX - 1)),
            dma((2,)), dma((2,)),
            dma((2, NZ - 1)), dma((2, NZ - 1)),
            dma((NC,)), dma((NC,)),
            dma((NC - 1,)), dma((NC - 1,)),
            dma((2, NC + 1)), dma((2, NC + 1)),
        ],
        compiler_params=pltpu.CompilerParams(
            collective_id=0, has_side_effects=True, vmem_limit_bytes=60 * 1024 * 1024
        ),
        name="key_rows",
    )(
        store_index,
        offsets,
        tenant,
        tokens,
        frozen_key_weight,
        store_a[0],
        store_b[0].T,
        bank_a,
        bank_b.T,
    )


def solution(mesh):
    in_specs = (
        P("rep", "tp"),
        P("rep"),
        P("rep"),
        P(),
        P("tp", None),
        P("rep", None, "tp"),
        P("rep", "tp", None),
        P(None, "tp"),
        P("tp", None),
    )
    return jax.shard_map(
        per_device, mesh=mesh, in_specs=in_specs, out_specs=P("rep", "tp"), check_vma=False
    )
```

time: 53.9 us -> 49.1 us (0.911)
  Pallas kernels: 49.6 us -> 46.1 us
  local copies, waits for them, and re-layouts: 2.79 us -> 1.54 us
    pallas_call x1, Pallas kernels: 49.6 us -> 46.1 us  [per_device(): pl.pallas_call(kernel, out_shape=jax.ShapeDtypeStruct((ROWS, HEAD), bf16)...]
    reshape x1 -> x0, local copies, waits for them, and re-layouts: 1.25 us -> none  [per_device(): tenant.reshape(1, ROWS)]
where the time goes in v2:
time: 49.1 us; the launch traced here: 48.9 us
  Pallas kernels  46.1 us (94%)
  local copies, waits for them, and re-layouts  1.54 us (3%)
  between operations  1.3 us (3%)
    pallas_call x1, Pallas kernels, per_device(): pl.pallas_call(kernel, out_shape=jax.ShapeDtypeStruct((ROWS, HEAD), bf16)...  46.1 us
    unnamed x1, local copies, waits for them, and re-layouts  1.54 us

profile of v2, /device:TPU:1, one launch (start us, length us, event | category | flops | bytes accessed | tf_op | source)
XLA Modules:
  0.0 48.9 jit_solution(11387789925248380694)
XLA Ops:
  1.3 46.1 %key_rows.1 = bf16[384,128]{1,0:T(8,128)(2,1)} custom-call(s32[1]{0:T(128)S(6)} %copy.12.index_ref, s32[1]{0:T(128)S(6)} %copy.11.offset_ref, s32[384]{0:T(512)} %tenant_ref.1, bf16[384,1536]{1,0:T(8,128)(2,1)} %tok_hbm.1, bf16[1536,1024]{1,0:T(8,128)(2,1)} %w_hbm.1, f32[64,1536]{1,0:T(8,128)} %bitcast.5, f32[64,128]{1,0:T(8,128)} %bitcast.6, ...), custom_call_target="tpu_custom_call" | custom-call | tf_op jit(solution)/shard_map/key_rows/pallas_call | solution.py:308
  47.4 1.5 %copy.13 = bf16[384,128]{1,0:T(8,128)(2,1)} copy(bf16[384,128]{1,0:T(8,128)(2,1)} %key_rows.1) | data formatting | bytes 196608

commit v3 on v2

--- a/solution.py
+++ b/solution.py
@@ -1,3 +1,4 @@
+import functools
 import math
 
 import jax
@@ -22,13 +23,15 @@
 
 
 def kernel(
-    index_ref, offset_ref, tenant_ref, tok_hbm, w_hbm, a_hbm, bt_hbm, ba_hbm, bbt_hbm, out_ref,
-    tok, w, a_raw, bt_raw, bank, ranks, bank_up, up,
-    z_src0, z_src1, z_got0, z_got1, x_got0, x_got1, y_got0, y_got1, g_got0, g_got1,
+    home,
+    index_hbm, offset_hbm, tenant_hbm, tok_hbm, w_hbm, a_hbm, bt_hbm, ba_hbm, bbt_hbm, out_ref,
+    index_ref, offset_ref, tenant_ref, tok, w, a_raw, bt_raw, bank, ranks, bank_up, up,
+    z_src0, z_src1, z_got0, z_got1, x_got0, x_got1, g_got0, g_got1,
     mine, pair_src, pair_got, part_src, part_got,
     l_mine, l_src, l_got, l_chip, l_chips, l_all,
     acc, cos2, sin2,
-    load_sem, z_ss, z_rs, x_ss, x_rs, y_ss, y_rs, g_ss, g_rs, q_ss, q_rs, p_ss, p_rs, l_ss, l_rs,
+    load_sem, ready,
+    z_ss, z_rs, x_ss, x_rs, y_ss, y_rs, g_ss, g_rs, q_ss, q_rs, p_ss, p_rs, l_ss, l_rs,
 ):
     bf16, f32 = jnp.bfloat16, jnp.float32
     rep, t = lax.axis_index("rep"), lax.axis_index("tp")
@@ -47,10 +50,15 @@
     c_peers = [(rep, 2 * q + core) for q in c_of]
     twin = (rep, 2 * yl + 1 - core)
 
+    at_home = yh == home
     barrier = pltpu.get_barrier_semaphore()
-    peers = z_peers + x_peers + [y_peer] + c_peers + [twin]
+    peers = z_peers + x_peers + c_peers + [twin]
     for peer in peers:
         pl.semaphore_signal(barrier, inc=1, device_id=peer, device_id_type=MESH)
+
+    @pl.when(yh == 0)
+    def _():
+        pl.semaphore_signal(barrier, inc=1, device_id=y_peer, device_id_type=MESH)
 
     bank_up[...] = jnp.zeros_like(bank_up)
     up[...] = jnp.zeros_like(up)
@@ -66,17 +74,17 @@
                 (w_hbm, w),
                 (bbt_hbm, bank_up.at[pl.ds(0, RANK), pl.ds(0, HEAD)]),
                 (bbt_hbm, bank_up.at[pl.ds(RANK, RANK), pl.ds(HEAD, HEAD)]),
+                (index_hbm, index_ref),
+                (offset_hbm, offset_ref),
+                (tenant_hbm, tenant_ref),
             ]
         )
     ]
     for load in loads:
         load.start()
 
-    root = index_ref[0]
-    root_y, root_z, root_x = root // (NZ * NX), (root // NX) % NZ, root % NX
-
-    z_src, z_got, x_got, y_got, g_got = (
-        (z_src0, z_src1), (z_got0, z_got1), (x_got0, x_got1), (y_got0, y_got1), (g_got0, g_got1)
+    z_src, z_got, x_got, g_got = (
+        (z_src0, z_src1), (z_got0, z_got1), (x_got0, x_got1), (g_got0, g_got1)
     )
 
     def tile(q, chunk, j):
@@ -95,14 +103,22 @@
                 row = 16 * (q // 2)
                 z_src[chunk][q, 48:64, :] = bt_raw[row : row + 16, :].astype(bf16)
 
-    pl.semaphore_wait(barrier, len(peers))
+    pl.semaphore_wait(barrier, len(peers) + yh)
+    if home == 0:
+
+        @pl.when(yh == 1)
+        def _():
+            pl.semaphore_signal(ready, inc=1, device_id=y_peer, device_id_type=MESH)
 
     started = []
 
-    def send(src, dst, ss, rs, peer):
-        copy = pltpu.make_async_remote_copy(
+    def remote(src, dst, ss, rs, peer):
+        return pltpu.make_async_remote_copy(
             src_ref=src, dst_ref=dst, send_sem=ss, recv_sem=rs, device_id=peer, device_id_type=MESH
         )
+
+    def send(*args):
+        copy = remote(*args)
         copy.start()
         started.append(copy)
         return copy
@@ -113,7 +129,7 @@
 
     z_copies = [
         [
-            send(
+            remote(
                 z_src[chunk].at[z_of[i]], z_got[chunk].at[z],
                 z_ss.at[chunk, i], z_rs.at[chunk, i], z_peers[i],
             )
@@ -121,8 +137,28 @@
         ]
         for chunk in range(2)
     ]
-    for chunk in range(2):
-        z_got[chunk][z] = z_src[chunk][z]
+    x_copies = [
+        [
+            remote(
+                x_got[chunk].at[x], x_got[chunk].at[x],
+                x_ss.at[chunk, i], x_rs.at[chunk, i], x_peers[i],
+            )
+            for i in range(NX - 1)
+        ]
+        for chunk in range(2)
+    ]
+    y_copies = [
+        remote(g_got[chunk].at[z], g_got[chunk].at[z], y_ss.at[chunk], y_rs.at[chunk], y_peer)
+        for chunk in range(2)
+    ]
+
+    @pl.when(at_home)
+    def _():
+        for chunk in range(2):
+            for copy in z_copies[chunk]:
+                copy.start()
+        for chunk in range(2):
+            z_got[chunk][z] = z_src[chunk][z]
 
     lane = lax.broadcasted_iota(jnp.int32, (PACK, HEAD), 1)
     left = lane < RANK
@@ -196,6 +232,7 @@
             passed(k - 1)
     passed(NC - 1)
 
+    loads[9].wait()
     wide = lax.broadcasted_iota(jnp.int32, (HALF, HEAD), 1)
     row = lax.broadcasted_iota(jnp.int32, (HALF, HEAD), 0)
     row = jnp.where(wide < HEAD // 2, row, row + HALF)
@@ -209,27 +246,27 @@
     sin2[0:HALF, :] = jnp.where(first, -sine, turned_sin)
     sin2[HALF:, :] = jnp.where(first, -turned_sin, sine)
 
-    x_copies, y_copies, g_copies = [], [], []
-    for chunk in range(2):
-        arrived(z_copies[chunk])
-        x_got[chunk][x] = z_got[chunk][root_z]
-        x_copies.append(
-            [
-                send(
-                    x_got[chunk].at[x], x_got[chunk].at[x],
-                    x_ss.at[chunk, i], x_rs.at[chunk, i], x_peers[i],
-                )
-                for i in range(NX - 1)
-            ]
-        )
-    for chunk in range(2):
-        arrived(x_copies[chunk])
-        y_got[chunk][yh] = x_got[chunk][root_x]
-        y_copies.append(
-            send(y_got[chunk].at[yh], y_got[chunk].at[yh], y_ss.at[chunk], y_rs.at[chunk], y_peer)
-        )
+    loads[8].wait()
+
+    @pl.when(at_home)
+    def _():
+        root = index_ref[0]
+        root_z, root_x = (root // NX) % NZ, root % NX
+        for chunk in range(2):
+            arrived(z_copies[chunk])
+            x_got[chunk][x] = z_got[chunk][root_z]
+            for copy in x_copies[chunk]:
+                copy.start()
+        for chunk in range(2):
+            arrived(x_copies[chunk])
+            g_got[chunk][z] = x_got[chunk][root_x]
+            if chunk == 0 and home == 0:
+                pl.semaphore_wait(ready, 1)
+            y_copies[chunk].start()
+
     bank_step = low_join(0, bank_step)
 
+    loads[10].wait()
     eye = lax.broadcasted_iota(jnp.int32, (HEAD, HEAD), 0) == lax.broadcasted_iota(
         jnp.int32, (HEAD, HEAD), 1
     )
@@ -245,9 +282,13 @@
         axis=0,
     )
 
+    g_copies = []
     for chunk in range(2):
-        y_copies[chunk].wait_recv()
-        g_got[chunk][z] = y_got[chunk][root_y]
+
+        @pl.when(jnp.logical_not(at_home))
+        def _(chunk=chunk):
+            y_copies[chunk].wait_recv()
+
         g_copies.append(
             [
                 send(
@@ -292,12 +333,14 @@
     for copy in started:
         copy.wait_send()
 
-
-def per_device(
-    tokens, tenant, offsets, store_index, frozen_key_weight, store_a, store_b, bank_a, bank_b
-):
+    @pl.when(at_home)
+    def _():
+        for copy in z_copies[0] + z_copies[1] + x_copies[0] + x_copies[1] + y_copies:
+            copy.wait_send()
+
+
+def key_rows(home, *args):
     bf16, f32 = jnp.bfloat16, jnp.float32
-    smem = pl.BlockSpec(memory_space=pltpu.SMEM)
     vmem = pl.BlockSpec(memory_space=pltpu.VMEM)
     hbm = pl.BlockSpec(memory_space=pl.ANY)
     dma = pltpu.SemaphoreType.DMA
@@ -306,11 +349,14 @@
         return [pltpu.VMEM((n, 16 * tiles, HEAD), bf16) for tiles in TILES]
 
     return pl.pallas_call(
-        kernel,
+        functools.partial(kernel, home),
         out_shape=jax.ShapeDtypeStruct((ROWS, HEAD), bf16),
-        in_specs=[smem, smem, vmem] + [hbm] * 6,
+        in_specs=[hbm] * 9,
         out_specs=vmem,
         scratch_shapes=[
+            pltpu.SMEM((1,), jnp.int32),
+            pltpu.SMEM((1,), jnp.int32),
+            pltpu.VMEM((ROWS,), jnp.int32),
             pltpu.VMEM((ROWS, FEAT), bf16),
             pltpu.VMEM((FEAT, 2 * NC * HEAD), bf16),
             pltpu.VMEM((RANK, FEAT), f32),
@@ -319,7 +365,7 @@
             pltpu.VMEM((2 * RANK, FEAT), bf16),
             pltpu.VMEM((2 * RANK, 2 * HEAD), bf16),
             pltpu.VMEM((2 * RANK, 2 * HEAD), bf16),
-            *slices(NZ), *slices(NZ), *slices(NX), *slices(NY), *slices(NZ),
+            *slices(NZ), *slices(NZ), *slices(NX), *slices(NZ),
             pltpu.VMEM((NC, ROWS, HEAD), f32),
             pltpu.VMEM((NC, ROWS, HEAD), bf16),
             pltpu.VMEM((NC, ROWS, HEAD), bf16),
@@ -334,7 +380,8 @@
             pltpu.VMEM((ROWS, HEAD), f32),
             pltpu.VMEM((ROWS, HEAD), f32),
             pltpu.VMEM((ROWS, HEAD), f32),
-            dma((8,)),
+            dma((11,)),
+            pltpu.SemaphoreType.REGULAR,
             dma((2, NZ - 1)), dma((2, NZ - 1)),
             dma((2, NX - 1)), dma((2, NX - 1)),
             dma((2,)), dma((2,)),
@@ -344,10 +391,19 @@
             dma((2, NC + 1)), dma((2, NC + 1)),
         ],
         compiler_params=pltpu.CompilerParams(
-            collective_id=0, has_side_effects=True, vmem_limit_bytes=60 * 1024 * 1024
+            collective_id=home, has_side_effects=True, vmem_limit_bytes=60 * 1024 * 1024
         ),
-        name="key_rows",
-    )(
+        name=f"key_rows_{home}",
+    )(*args)
+
+
+def per_device(
+    tokens, tenant, offsets, store_index, frozen_key_weight, store_a, store_b, bank_a, bank_b
+):
+    return lax.cond(
+        store_index[0] < NZ * NX,
+        functools.partial(key_rows, 0),
+        functools.partial(key_rows, 1),
         store_index,
         offsets,
         tenant,

time: 49.1 us -> 47.5 us (0.967)
  local copies, waits for them, and re-layouts: 1.54 us -> 0.64 us
  between operations: 1.3 us -> 0.66 us
    unnamed x1, local copies, waits for them, and re-layouts: 1.54 us -> 0.64 us
where the time goes in v3:
time: 47.5 us; the launch traced here: 47.3 us
  Pallas kernels  46 us (97%)
  between operations  0.66 us (1%)
  local copies, waits for them, and re-layouts  0.64 us (1%)
    pallas_call x1, Pallas kernels, key_rows(): pl.pallas_call(functools.partial(kernel, home), out_shape=jax.ShapeDtypeS...  46 us

profile of v3, /device:TPU:1, one launch (start us, length us, event | category | flops | bytes accessed | tf_op | source)
XLA Modules:
  0.0 47.3 jit_solution(8558419763255648428)
XLA Ops:
  0.7 46.0 %conditional.1 = (bf16[384,128]{1,0:T(8,128)(2,1)S(1)}) conditional(s32[]{:T(128)} %bitcast.2, (s32[1]{0:T(128)}, s32[1]{0:T(128)}, s32[384]{0:T(512)}, bf16[384,1536]{1,0:T(8,128)(2,1)}, bf16[1536,1024]{1,0:T(8,128)(2,1)}, /*index=5*/f32[1,64,1536]{2,1,0:T(8,128)}, f32[64,128]{1,0:T(8,128)}, bf16[64,1536]{1,0:T(8,128)(2,1)}, ...), branch_computations={%region_0.0_spmd, %region_1.0_spmd} | conditional | bytes 8 | solution.py:403
  0.7 46.0 %key_rows_1.1 = bf16[384,128]{1,0:T(8,128)(2,1)S(1)} custom-call(s32[1]{0:T(128)} %get-tuple-element.44.index_hbm, s32[1]{0:T(128)} %get-tuple-element.75.offset_hbm, s32[384]{0:T(512)} %get-tuple-element.77.tenant_hbm, bf16[384,1536]{1,0:T(8,128)(2,1)} %get-tuple-element.79.tok_hbm, bf16[1536,1024]{1,0:T(8,128)(2,1)} %get-tuple-element.81.w_hbm, ...), custom_call_target="tpu_custom_call" | custom-call | tf_op jit(solution)/shard_map/cond/branch_0_fun/key_rows_1/pallas_call | solution.py:351
  46.7 0.6 %copy.28 = bf16[384,128]{1,0:T(8,128)(2,1)} copy(bf16[384,128]{1,0:T(8,128)(2,1)S(1)} %get-tuple-element.62) | data formatting | bytes 196608

commit v4 on v3

--- a/solution.py
+++ b/solution.py
@@ -18,20 +18,23 @@
 RANK = 64
 HALF = ROWS // 2
 PACK = ROWS // 4
-TILES = (4, 3)
+NH = 4
+NL = NZ - NH
+WIDE = 6
+TILES = (WIDE + 1, WIDE)
 CHUNK = FEAT // 2
 
 
 def kernel(
-    home,
+    root_z,
     index_hbm, offset_hbm, tenant_hbm, tok_hbm, w_hbm, a_hbm, bt_hbm, ba_hbm, bbt_hbm, out_ref,
     index_ref, offset_ref, tenant_ref, tok, w, a_raw, bt_raw, bank, ranks, bank_up, up,
-    z_src0, z_src1, z_got0, z_got1, x_got0, x_got1, g_got0, g_got1,
+    src0, src1, x_got0, x_got1, y_got0, y_got1, g_got0, g_got1,
     mine, pair_src, pair_got, part_src, part_got,
     l_mine, l_src, l_got, l_chip, l_chips, l_all,
     acc, cos2, sin2,
     load_sem, ready,
-    z_ss, z_rs, x_ss, x_rs, y_ss, y_rs, g_ss, g_rs, q_ss, q_rs, p_ss, p_rs, l_ss, l_rs,
+    h_ss, h_rs, x_ss, x_rs, y_ss, y_rs, g_ss, g_rs, q_ss, q_rs, p_ss, p_rs, l_ss, l_rs,
 ):
     bf16, f32 = jnp.bfloat16, jnp.float32
     rep, t = lax.axis_index("rep"), lax.axis_index("tp")
@@ -41,24 +44,29 @@
     def at(yh_, z_, x_):
         return (yh_ * NZ + z_) * NX + x_
 
-    z_of = [(z + k) % NZ for k in range(1, NZ)]
     x_of = [(x + k) % NX for k in range(1, NX)]
     c_of = [(yl + k) % NC for k in range(1, NC)]
-    z_peers = [(at(yh, q, x), t) for q in z_of]
+    holder, source = z < NH, z == root_z
+    h_of = [(z + k) % NH for k in range(1, NH)]
+    h_peers = [(at(yh, q, x), t) for q in h_of]
+    holders = [(at(yh, q, x), t) for q in range(NH)]
+    late_peers = [(at(yh, NH + q, x), t) for q in range(NL)]
     x_peers = [(at(yh, z, q), t) for q in x_of]
     y_peer = (at(1 - yh, z, x), t)
     c_peers = [(rep, 2 * q + core) for q in c_of]
     twin = (rep, 2 * yl + 1 - core)
 
-    at_home = yh == home
     barrier = pltpu.get_barrier_semaphore()
-    peers = z_peers + x_peers + c_peers + [twin]
-    for peer in peers:
-        pl.semaphore_signal(barrier, inc=1, device_id=peer, device_id_type=MESH)
-
-    @pl.when(yh == 0)
-    def _():
-        pl.semaphore_signal(barrier, inc=1, device_id=y_peer, device_id_type=MESH)
+
+    def greet(peers):
+        for peer in peers:
+            pl.semaphore_signal(barrier, inc=1, device_id=peer, device_id_type=MESH)
+
+    greet(c_peers + [twin])
+
+    @pl.when(holder)
+    def _():
+        greet(h_peers + x_peers + [y_peer] + late_peers)
 
     bank_up[...] = jnp.zeros_like(bank_up)
     up[...] = jnp.zeros_like(up)
@@ -66,8 +74,6 @@
         pltpu.make_async_copy(src, dst, load_sem.at[i])
         for i, (src, dst) in enumerate(
             [
-                (a_hbm, a_raw),
-                (bt_hbm, bt_raw),
                 (tok_hbm, tok),
                 (ba_hbm, bank.at[pl.ds(0, RANK)]),
                 (ba_hbm, bank.at[pl.ds(RANK, RANK)]),
@@ -77,38 +83,47 @@
                 (index_hbm, index_ref),
                 (offset_hbm, offset_ref),
                 (tenant_hbm, tenant_ref),
+                (a_hbm, a_raw),
+                (bt_hbm, bt_raw),
             ]
         )
     ]
-    for load in loads:
+
+    @pl.when(source)
+    def _():
+        for load in loads[9:]:
+            load.start()
+
+    for load in loads[:9]:
         load.start()
 
-    z_src, z_got, x_got, g_got = (
-        (z_src0, z_src1), (z_got0, z_got1), (x_got0, x_got1), (g_got0, g_got1)
-    )
-
-    def tile(q, chunk, j):
-        return 16 * (q // 2), chunk * CHUNK + ((q % 2) * 3 + j) * HEAD
-
-    loads[0].wait()
-    loads[1].wait()
-    for chunk in range(2):
-        for q in range(NZ):
-            for j in range(3):
-                row, column = tile(q, chunk, j)
-                z_src[chunk][q, 16 * j : 16 * (j + 1), :] = a_raw[
-                    row : row + 16, column : column + HEAD
-                ].astype(bf16)
-            if chunk == 0:
-                row = 16 * (q // 2)
-                z_src[chunk][q, 48:64, :] = bt_raw[row : row + 16, :].astype(bf16)
-
-    pl.semaphore_wait(barrier, len(peers) + yh)
-    if home == 0:
-
-        @pl.when(yh == 1)
-        def _():
-            pl.semaphore_signal(ready, inc=1, device_id=y_peer, device_id_type=MESH)
+    src, x_got, y_got, g_got = (
+        (src0, src1), (x_got0, x_got1), (y_got0, y_got1), (g_got0, g_got1)
+    )
+
+    @pl.when(source)
+    def _():
+        for load in loads[9:]:
+            load.wait()
+        for chunk in range(2):
+            for h in range(NH):
+                for j in range(WIDE):
+                    column = chunk * CHUNK + j * HEAD
+                    src[chunk][h, 16 * j : 16 * (j + 1), :] = a_raw[
+                        16 * h : 16 * (h + 1), column : column + HEAD
+                    ].astype(bf16)
+                if chunk == 0:
+                    src[chunk][h, 16 * WIDE :, :] = bt_raw[16 * h : 16 * (h + 1), :].astype(bf16)
+            if root_z < NH:
+                x_got[chunk][x] = src[chunk][root_z]
+
+    replica = NC
+    pl.semaphore_wait(barrier, replica + jnp.where(holder, NH + NX - 1, NH))
+
+    @pl.when(jnp.logical_not(holder))
+    def _():
+        for peer in holders:
+            pl.semaphore_signal(ready.at[z - NH], inc=1, device_id=peer, device_id_type=MESH)
 
     started = []
 
@@ -127,13 +142,13 @@
         for copy in copies:
             copy.wait_recv()
 
-    z_copies = [
+    far = [h for h in range(NH) if h != root_z]
+    h_copies = [
         [
             remote(
-                z_src[chunk].at[z_of[i]], z_got[chunk].at[z],
-                z_ss.at[chunk, i], z_rs.at[chunk, i], z_peers[i],
+                src[chunk].at[h], x_got[chunk].at[x], h_ss.at[chunk, h], h_rs.at[chunk], holders[h]
             )
-            for i in range(NZ - 1)
+            for h in far
         ]
         for chunk in range(2)
     ]
@@ -148,17 +163,24 @@
         for chunk in range(2)
     ]
     y_copies = [
-        remote(g_got[chunk].at[z], g_got[chunk].at[z], y_ss.at[chunk], y_rs.at[chunk], y_peer)
+        remote(y_got[chunk].at[yh], y_got[chunk].at[yh], y_ss.at[chunk], y_rs.at[chunk], y_peer)
         for chunk in range(2)
     ]
 
-    @pl.when(at_home)
-    def _():
-        for chunk in range(2):
-            for copy in z_copies[chunk]:
+    def g_copies(chunk, first, peers):
+        return [
+            remote(
+                g_got[chunk].at[z], g_got[chunk].at[z],
+                g_ss.at[chunk, first + i], g_rs.at[chunk, z], peer,
+            )
+            for i, peer in enumerate(peers)
+        ]
+
+    @pl.when(source)
+    def _():
+        for chunk in range(2):
+            for copy in h_copies[chunk]:
                 copy.start()
-        for chunk in range(2):
-            z_got[chunk][z] = z_src[chunk][z]
 
     lane = lax.broadcasted_iota(jnp.int32, (PACK, HEAD), 1)
     left = lane < RANK
@@ -199,12 +221,12 @@
     def times_ranks(a, b):
         return lax.dot_general(a, b, (((1,), (1,)), ((), ())), preferred_element_type=f32)
 
+    loads[0].wait()
+    loads[1].wait()
     loads[2].wait()
+    bank_step = low_start(0, times_ranks(tok[...], bank[...]))
+
     loads[3].wait()
-    loads[4].wait()
-    bank_step = low_start(0, times_ranks(tok[...], bank[...]))
-
-    loads[5].wait()
     order = c_of + [yl]
     pair_copies = []
     part_copies = []
@@ -232,7 +254,7 @@
             passed(k - 1)
     passed(NC - 1)
 
-    loads[9].wait()
+    loads[7].wait()
     wide = lax.broadcasted_iota(jnp.int32, (HALF, HEAD), 1)
     row = lax.broadcasted_iota(jnp.int32, (HALF, HEAD), 0)
     row = jnp.where(wide < HEAD // 2, row, row + HALF)
@@ -246,27 +268,27 @@
     sin2[0:HALF, :] = jnp.where(first, -sine, turned_sin)
     sin2[HALF:, :] = jnp.where(first, -turned_sin, sine)
 
-    loads[8].wait()
-
-    @pl.when(at_home)
-    def _():
-        root = index_ref[0]
-        root_z, root_x = (root // NX) % NZ, root % NX
-        for chunk in range(2):
-            arrived(z_copies[chunk])
-            x_got[chunk][x] = z_got[chunk][root_z]
+    loads[6].wait()
+
+    @pl.when(holder)
+    def _():
+        root_x = index_ref[0] % NX
+        for chunk in range(2):
+
+            @pl.when(jnp.logical_not(source))
+            def _(chunk=chunk):
+                h_copies[chunk][0].wait_recv()
+
             for copy in x_copies[chunk]:
                 copy.start()
         for chunk in range(2):
             arrived(x_copies[chunk])
-            g_got[chunk][z] = x_got[chunk][root_x]
-            if chunk == 0 and home == 0:
-                pl.semaphore_wait(ready, 1)
+            y_got[chunk][yh] = x_got[chunk][root_x]
             y_copies[chunk].start()
 
     bank_step = low_join(0, bank_step)
 
-    loads[10].wait()
+    loads[8].wait()
     eye = lax.broadcasted_iota(jnp.int32, (HEAD, HEAD), 0) == lax.broadcasted_iota(
         jnp.int32, (HEAD, HEAD), 1
     )
@@ -282,47 +304,51 @@
         axis=0,
     )
 
-    g_copies = []
-    for chunk in range(2):
-
-        @pl.when(jnp.logical_not(at_home))
-        def _(chunk=chunk):
+    @pl.when(holder)
+    def _():
+        root_y = index_ref[0] // (NZ * NX)
+        for chunk in range(2):
             y_copies[chunk].wait_recv()
-
-        g_copies.append(
-            [
-                send(
-                    g_got[chunk].at[z], g_got[chunk].at[z],
-                    g_ss.at[chunk, i], g_rs.at[chunk, i], z_peers[i],
-                )
-                for i in range(NZ - 1)
-            ]
-        )
+            g_got[chunk][z] = y_got[chunk][root_y]
+            for copy in g_copies(chunk, 0, h_peers):
+                copy.start()
+        for i in range(NL):
+            pl.semaphore_wait(ready.at[i], 1)
+        for chunk in range(2):
+            for copy in g_copies(chunk, NH - 1, late_peers):
+                copy.start()
 
     total = acc[...]
     for k, copy in enumerate(part_copies):
         copy.wait_recv()
         total = total + part_got[k].astype(f32)
-    loads[6].wait()
-    loads[7].wait()
+    loads[4].wait()
+    loads[5].wait()
     acc[...] = total + jnp.where(tenant == 1.0, expanded(0, bank_step, bank_up), 0.0)
 
     low = None
     for chunk in range(2):
-        arrived(g_copies[chunk])
-        for q in range(NZ):
-            for j in range(3):
-                row, column = tile(q, chunk, j)
-                value = g_got[chunk][q, 16 * j : 16 * (j + 1), :]
-                ranks[row : row + 16, column : column + HEAD] = value
-                ranks[RANK + row : RANK + row + 16, column : column + HEAD] = value
+        for h in range(NH):
+
+            @pl.when(z != h)
+            def _(chunk=chunk, h=h):
+                remote(
+                    g_got[chunk].at[h], g_got[chunk].at[h],
+                    g_ss.at[chunk, 0], g_rs.at[chunk, h], y_peer,
+                ).wait_recv()
+
+            for j in range(WIDE):
+                column = chunk * CHUNK + j * HEAD
+                value = g_got[chunk][h, 16 * j : 16 * (j + 1), :]
+                for row in (16 * h, RANK + 16 * h):
+                    ranks[row : row + 16, column : column + HEAD] = value
         columns = slice(chunk * CHUNK, (chunk + 1) * CHUNK)
         term = times_ranks(tok[:, columns], ranks[:, columns])
         low = term if low is None else low + term
     store_step = low_start(1, low)
-    for q in range(0, NZ, 2):
-        row = 16 * (q // 2)
-        value = g_got[0][q, 48:64, :]
+    for h in range(NH):
+        row = 16 * h
+        value = g_got[0][h, 16 * WIDE :, :]
         up[row : row + 16, 0:HEAD] = value
         up[RANK + row : RANK + row + 16, HEAD:] = value
     store_step = low_spread(1, store_step)
@@ -333,13 +359,19 @@
     for copy in started:
         copy.wait_send()
 
-    @pl.when(at_home)
-    def _():
-        for copy in z_copies[0] + z_copies[1] + x_copies[0] + x_copies[1] + y_copies:
+    @pl.when(source)
+    def _():
+        for copy in h_copies[0] + h_copies[1]:
             copy.wait_send()
 
-
-def key_rows(home, *args):
+    @pl.when(holder)
+    def _():
+        for chunk in range(2):
+            for copy in x_copies[chunk] + [y_copies[chunk]] + g_copies(chunk, 0, h_peers + late_peers):
+                copy.wait_send()
+
+
+def key_rows(root_z, *args):
     bf16, f32 = jnp.bfloat16, jnp.float32
     vmem = pl.BlockSpec(memory_space=pltpu.VMEM)
     hbm = pl.BlockSpec(memory_space=pl.ANY)
@@ -349,7 +381,7 @@
         return [pltpu.VMEM((n, 16 * tiles, HEAD), bf16) for tiles in TILES]
 
     return pl.pallas_call(
-        functools.partial(kernel, home),
+        functools.partial(kernel, root_z),
         out_shape=jax.ShapeDtypeStruct((ROWS, HEAD), bf16),
         in_specs=[hbm] * 9,
         out_specs=vmem,
@@ -365,7 +397,7 @@
             pltpu.VMEM((2 * RANK, FEAT), bf16),
             pltpu.VMEM((2 * RANK, 2 * HEAD), bf16),
             pltpu.VMEM((2 * RANK, 2 * HEAD), bf16),
-            *slices(NZ), *slices(NZ), *slices(NX), *slices(NZ),
+            *slices(NH), *slices(NX), *slices(NY), *slices(NH),
             pltpu.VMEM((NC, ROWS, HEAD), f32),
             pltpu.VMEM((NC, ROWS, HEAD), bf16),
             pltpu.VMEM((NC, ROWS, HEAD), bf16),
@@ -381,29 +413,28 @@
             pltpu.VMEM((ROWS, HEAD), f32),
             pltpu.VMEM((ROWS, HEAD), f32),
             dma((11,)),
-            pltpu.SemaphoreType.REGULAR,
-            dma((2, NZ - 1)), dma((2, NZ - 1)),
+            pltpu.SemaphoreType.REGULAR((NL,)),
+            dma((2, NH)), dma((2,)),
             dma((2, NX - 1)), dma((2, NX - 1)),
             dma((2,)), dma((2,)),
-            dma((2, NZ - 1)), dma((2, NZ - 1)),
+            dma((2, NZ - 1)), dma((2, NH)),
             dma((NC,)), dma((NC,)),
             dma((NC - 1,)), dma((NC - 1,)),
             dma((2, NC + 1)), dma((2, NC + 1)),
         ],
         compiler_params=pltpu.CompilerParams(
-            collective_id=home, has_side_effects=True, vmem_limit_bytes=60 * 1024 * 1024
+            collective_id=root_z, has_side_effects=True, vmem_limit_bytes=60 * 1024 * 1024
         ),
-        name=f"key_rows_{home}",
+        name=f"key_rows_{root_z}",
     )(*args)
 
 
 def per_device(
     tokens, tenant, offsets, store_index, frozen_key_weight, store_a, store_b, bank_a, bank_b
 ):
-    return lax.cond(
-        store_index[0] < NZ * NX,
-        functools.partial(key_rows, 0),
-        functools.partial(key_rows, 1),
+    return lax.switch(
+        lax.rem(lax.div(store_index[0], NX), NZ),
+        [functools.partial(key_rows, z) for z in range(NZ)],
         store_index,
         offsets,
         tenant,

time: 47.5 us -> 44.6 us (0.939)
  Pallas kernels: 46 us -> 42.6 us
  loops' own time: 0.02 us -> 0.56 us
    pallas_call x1, Pallas kernels: 46 us -> 42.6 us  [key_rows(): pl.pallas_call(functools.partial(kernel, root_z), out_shape=jax.ShapeDtyp...]
    another operation x1, loops' own time: 0.02 us -> 0.56 us  [per_device(): lax.switch(lax.rem(lax.div(store_index[0], NX), NZ), [functools.partial(k...]
where the time goes in v4:
time: 44.6 us; the launch traced here: 44.5 us
  Pallas kernels  42.6 us (96%)
  between operations  0.68 us (2%)
  local copies, waits for them, and re-layouts  0.64 us (1%)
  loops' own time  0.56 us (1%)
    pallas_call x1, Pallas kernels, key_rows(): pl.pallas_call(functools.partial(kernel, root_z), out_shape=jax.ShapeDtyp...  42.6 us

profile of v4, /device:TPU:1, one launch (start us, length us, event | category | flops | bytes accessed | tf_op | source)
XLA Modules:
  0.0 44.5 jit_solution(5852515480817965712)
XLA Ops:
  0.7 43.2 %conditional.1 = (bf16[384,128]{1,0:T(8,128)(2,1)S(1)}) conditional(s32[]{:T(128)} %clamp.3, (s32[1]{0:T(128)}, s32[1]{0:T(128)}, s32[384]{0:T(512)}, bf16[384,1536]{1,0:T(8,128)(2,1)}, bf16[1536,1024]{1,0:T(8,128)(2,1)}, /*index=5*/f32[1,64,1536]{2,1,0:T(8,128)}, f32[64,128]{1,0:T(8,128)}, ...), branch_computations={%region_0.0_spmd, %region_1.0_spmd, %region_2.0_spmd, %region_3.0_... | conditional | bytes 8 | solution.py:435
  0.9 42.6 %key_rows_6.1 = bf16[384,128]{1,0:T(8,128)(2,1)S(1)} custom-call(s32[1]{0:T(128)} %get-tuple-element.212.index_hbm, s32[1]{0:T(128)} %get-tuple-element.285.offset_hbm, s32[384]{0:T(512)} %get-tuple-element.293.tenant_hbm, bf16[384,1536]{1,0:T(8,128)(2,1)} %get-tuple-element.301.tok_hbm, bf16[1536,1024]{1,0:T(8,128)(2,1)} %get-tuple-element.309.w_hbm, ...), custom_call_target="tpu_custom_call" | custom-call | tf_op jit(solution)/shard_map/cond/branch_6_fun/key_rows_6/pallas_call | solution.py:383
  43.8 0.6 %copy.76 = bf16[384,128]{1,0:T(8,128)(2,1)} copy(bf16[384,128]{1,0:T(8,128)(2,1)S(1)} %get-tuple-element.230) | data formatting | bytes 196608

commit v5 on v4

--- a/solution.py
+++ b/solution.py
@@ -20,6 +20,7 @@
 PACK = ROWS // 4
 NH = 4
 NL = NZ - NH
+EARLY = 0
 WIDE = 6
 TILES = (WIDE + 1, WIDE)
 CHUNK = FEAT // 2
@@ -100,30 +101,6 @@
     src, x_got, y_got, g_got = (
         (src0, src1), (x_got0, x_got1), (y_got0, y_got1), (g_got0, g_got1)
     )
-
-    @pl.when(source)
-    def _():
-        for load in loads[9:]:
-            load.wait()
-        for chunk in range(2):
-            for h in range(NH):
-                for j in range(WIDE):
-                    column = chunk * CHUNK + j * HEAD
-                    src[chunk][h, 16 * j : 16 * (j + 1), :] = a_raw[
-                        16 * h : 16 * (h + 1), column : column + HEAD
-                    ].astype(bf16)
-                if chunk == 0:
-                    src[chunk][h, 16 * WIDE :, :] = bt_raw[16 * h : 16 * (h + 1), :].astype(bf16)
-            if root_z < NH:
-                x_got[chunk][x] = src[chunk][root_z]
-
-    replica = NC
-    pl.semaphore_wait(barrier, replica + jnp.where(holder, NH + NX - 1, NH))
-
-    @pl.when(jnp.logical_not(holder))
-    def _():
-        for peer in holders:
-            pl.semaphore_signal(ready.at[z - NH], inc=1, device_id=peer, device_id_type=MESH)
 
     started = []
 
@@ -176,12 +153,6 @@
             for i, peer in enumerate(peers)
         ]
 
-    @pl.when(source)
-    def _():
-        for chunk in range(2):
-            for copy in h_copies[chunk]:
-                copy.start()
-
     lane = lax.broadcasted_iota(jnp.int32, (PACK, HEAD), 1)
     left = lane < RANK
 
@@ -192,6 +163,8 @@
         ]
         l_mine[s] = jnp.where(core == 0, halves[0], halves[1])
         l_src[s] = jnp.where(core == 0, halves[1], halves[0]).astype(bf16)
+
+    def low_swap(s):
         return send(l_src.at[s], l_got.at[s], l_ss.at[s, 0], l_rs.at[s, 0], twin)
 
     def low_spread(s, copy):
@@ -221,38 +194,50 @@
     def times_ranks(a, b):
         return lax.dot_general(a, b, (((1,), (1,)), ((), ())), preferred_element_type=f32)
 
+    def greeted():
+        replica = NC
+        pl.semaphore_wait(barrier, replica + jnp.where(holder, NH + NX - 1, NH))
+
+    def cut():
+        for load in loads[9:]:
+            load.wait()
+        for chunk in range(2):
+            for h in range(NH):
+                for j in range(WIDE):
+                    column = chunk * CHUNK + j * HEAD
+                    src[chunk][h, 16 * j : 16 * (j + 1), :] = a_raw[
+                        16 * h : 16 * (h + 1), column : column + HEAD
+                    ].astype(bf16)
+                if chunk == 0:
+                    src[chunk][h, 16 * WIDE :, :] = bt_raw[16 * h : 16 * (h + 1), :].astype(bf16)
+            if root_z < NH:
+                x_got[chunk][x] = src[chunk][root_z]
+
+    def push():
+        for chunk in range(2):
+            for copy in h_copies[chunk]:
+                copy.start()
+
+    source_first = root_z >= NH - 1
+    if source_first:
+
+        @pl.when(source)
+        def _():
+            cut()
+            greeted()
+            push()
+
     loads[0].wait()
     loads[1].wait()
     loads[2].wait()
-    bank_step = low_start(0, times_ranks(tok[...], bank[...]))
-
+    low_start(0, times_ranks(tok[...], bank[...]))
     loads[3].wait()
     order = c_of + [yl]
-    pair_copies = []
-    part_copies = []
-
-    def passed(k):
-        pair_copies[k].wait_recv()
-        total = mine[k] + pair_got[k].astype(f32)
-        if k == NC - 1:
-            acc[...] = total
-            return
-        part_src[k] = total.astype(bf16)
-        part_copies.append(
-            send(part_src.at[k], part_got.at[k], p_ss.at[k], p_rs.at[k], c_peers[k])
-        )
-
     for k, q in enumerate(order):
         column = pl.multiple_of(q * 2 * HEAD, 2 * HEAD)
         both = jnp.dot(tok[...], w[:, pl.ds(column, 2 * HEAD)], preferred_element_type=f32)
         mine[k] = jnp.where(core == 0, both[:, :HEAD], both[:, HEAD:])
         pair_src[k] = jnp.where(core == 0, both[:, HEAD:], both[:, :HEAD]).astype(bf16)
-        pair_copies.append(send(pair_src.at[k], pair_got.at[k], q_ss.at[k], q_rs.at[k], twin))
-        if k == 1:
-            bank_step = low_spread(0, bank_step)
-        if k >= 1:
-            passed(k - 1)
-    passed(NC - 1)
 
     loads[7].wait()
     wide = lax.broadcasted_iota(jnp.int32, (HALF, HEAD), 1)
@@ -268,26 +253,6 @@
     sin2[0:HALF, :] = jnp.where(first, -sine, turned_sin)
     sin2[HALF:, :] = jnp.where(first, -turned_sin, sine)
 
-    loads[6].wait()
-
-    @pl.when(holder)
-    def _():
-        root_x = index_ref[0] % NX
-        for chunk in range(2):
-
-            @pl.when(jnp.logical_not(source))
-            def _(chunk=chunk):
-                h_copies[chunk][0].wait_recv()
-
-            for copy in x_copies[chunk]:
-                copy.start()
-        for chunk in range(2):
-            arrived(x_copies[chunk])
-            y_got[chunk][yh] = x_got[chunk][root_x]
-            y_copies[chunk].start()
-
-    bank_step = low_join(0, bank_step)
-
     loads[8].wait()
     eye = lax.broadcasted_iota(jnp.int32, (HEAD, HEAD), 0) == lax.broadcasted_iota(
         jnp.int32, (HEAD, HEAD), 1
@@ -304,6 +269,69 @@
         axis=0,
     )
 
+    if source_first:
+
+        @pl.when(jnp.logical_not(source))
+        def _():
+            greeted()
+    else:
+
+        @pl.when(source)
+        def _():
+            cut()
+
+        greeted()
+
+        @pl.when(source)
+        def _():
+            push()
+
+    @pl.when(jnp.logical_not(holder))
+    def _():
+        for peer in holders:
+            pl.semaphore_signal(ready.at[z - NH], inc=1, device_id=peer, device_id_type=MESH)
+
+    bank_step = low_swap(0)
+    pair_copies = [
+        send(pair_src.at[k], pair_got.at[k], q_ss.at[k], q_rs.at[k], twin) for k in range(NC)
+    ]
+    bank_step = low_spread(0, bank_step)
+
+    def part(k):
+        return send(part_src.at[k], part_got.at[k], p_ss.at[k], p_rs.at[k], c_peers[k])
+
+    part_copies = []
+    for k, copy in enumerate(pair_copies):
+        copy.wait_recv()
+        total = mine[k] + pair_got[k].astype(f32)
+        if k == NC - 1:
+            acc[...] = total
+        else:
+            part_src[k] = total.astype(bf16)
+            if k < EARLY:
+                part_copies.append(part(k))
+
+    loads[6].wait()
+
+    @pl.when(holder)
+    def _():
+        root_x = index_ref[0] % NX
+        for chunk in range(2):
+
+            @pl.when(jnp.logical_not(source))
+            def _(chunk=chunk):
+                h_copies[chunk][0].wait_recv()
+
+            for copy in x_copies[chunk]:
+                copy.start()
+        for chunk in range(2):
+            arrived(x_copies[chunk])
+            y_got[chunk][yh] = x_got[chunk][root_x]
+            y_copies[chunk].start()
+
+    part_copies += [part(k) for k in range(EARLY, NC - 1)]
+    bank_step = low_join(0, bank_step)
+
     @pl.when(holder)
     def _():
         root_y = index_ref[0] // (NZ * NX)
@@ -345,7 +373,8 @@
         columns = slice(chunk * CHUNK, (chunk + 1) * CHUNK)
         term = times_ranks(tok[:, columns], ranks[:, columns])
         low = term if low is None else low + term
-    store_step = low_start(1, low)
+    low_start(1, low)
+    store_step = low_swap(1)
     for h in range(NH):
         row = 16 * h
         value = g_got[0][h, 16 * WIDE :, :]

time: 44.6 us -> 41.8 us (0.937)
  Pallas kernels: 42.6 us -> 39.8 us
    pallas_call x1, Pallas kernels: 42.6 us -> 39.8 us  [key_rows(): pl.pallas_call(functools.partial(kernel, root_z), out_shape=jax.ShapeDtyp...]
where the time goes in v5:
time: 41.8 us; the launch traced here: 41.7 us
  Pallas kernels  39.8 us (95%)
  between operations  0.68 us (2%)
  local copies, waits for them, and re-layouts  0.64 us (2%)
  loops' own time  0.57 us (1%)
    pallas_call x1, Pallas kernels, key_rows(): pl.pallas_call(functools.partial(kernel, root_z), out_shape=jax.ShapeDtyp...  39.8 us

profile of v5, /device:TPU:1, one launch (start us, length us, event | category | flops | bytes accessed | tf_op | source)
XLA Modules:
  0.0 41.7 jit_solution(104205957264025910)
XLA Ops:
  0.7 40.4 %conditional.1 = (bf16[384,128]{1,0:T(8,128)(2,1)S(1)}) conditional(s32[]{:T(128)} %clamp.3, (s32[1]{0:T(128)}, s32[1]{0:T(128)}, s32[384]{0:T(512)}, bf16[384,1536]{1,0:T(8,128)(2,1)}, bf16[1536,1024]{1,0:T(8,128)(2,1)}, /*index=5*/f32[1,64,1536]{2,1,0:T(8,128)}, f32[64,128]{1,0:T(8,128)}, ...), branch_computations={%region_0.0_spmd, %region_1.0_spmd, %region_2.0_spmd, %region_3.0_... | conditional | bytes 8 | solution.py:464
  0.7 39.8 %key_rows_1.1 = bf16[384,128]{1,0:T(8,128)(2,1)S(1)} custom-call(s32[1]{0:T(128)} %get-tuple-element.167.index_hbm, s32[1]{0:T(128)} %get-tuple-element.280.offset_hbm, s32[384]{0:T(512)} %get-tuple-element.288.tenant_hbm, bf16[384,1536]{1,0:T(8,128)(2,1)} %get-tuple-element.296.tok_hbm, bf16[1536,1024]{1,0:T(8,128)(2,1)} %get-tuple-element.304.w_hbm, ...), custom_call_target="tpu_custom_call" | custom-call | tf_op jit(solution)/shard_map/cond/branch_1_fun/key_rows_1/pallas_call | solution.py:412
  41.1 0.6 %copy.76 = bf16[384,128]{1,0:T(8,128)(2,1)} copy(bf16[384,128]{1,0:T(8,128)(2,1)S(1)} %get-tuple-element.230) | data formatting | bytes 196608
